TPU v7x, 256 devices: a whole 4x4x8 slice. The times are simulated.
256 devices in a mesh: seq: 8 (over z), head: 32 (over x, y, core).
Axes of the slice: x: 4, y: 4, z: 8, core: 2. Of those that a mesh axis runs over, the one named last changes fastest.
Arguments:
- projected: bfloat16 [2, 16384, 16384], P(None, ('seq', 'head')), may hold values from -6 to 6
- state_maps: bfloat16 [2, 16384, 4096], P(None, ('seq', 'head')), may hold values from -3 to 3
- step_raw: bfloat16 [2, 16384, 256], P(None, ('seq', 'head')), may hold values from -3 to 14
- step_bias: float32 [256], P('head'), may hold values from -9 to -2
- decay_rate: float32 [256], P('head'), may hold values from 0.1 to 2
- skip_gain: float32 [256], P('head'), may hold values from 0.5 to 1.5
- conv_weight: bfloat16 [4, 16384], P(None, 'head'), may hold values from -3 to 3
- conv_bias: float32 [16384], P('head'), may hold values from -1.5 to 1.5
- map_weight: bfloat16 [4, 4096], replicated, may hold values from -3 to 3
- map_bias: float32 [4096], replicated, may hold values from -1.5 to 1.5
Outputs:
- mixed_out: bfloat16 [2, 16384, 16384], P(None, ('seq', 'head'))
All inputs are finite; a program needn't handle non-finite values.
Results may differ from a plain program's by a relative error of at most 0.0057.
Values may be sent and summed in bfloat16 or wider, within the bound.
A program may use at most 128 MiB of HBM per device.

v0:
```python
import jax
import jax.numpy as jnp
from jax import lax
from jax.sharding import PartitionSpec as P

HEAD_DIM = 64
STATE = 256
GROUPS = 8
SPAN = 256
CONV = 4


def from_behind(array, axis, by):
    count = lax.axis_size(axis)
    pairs = [(i, i + by) for i in range(count) if 0 <= i + by < count]
    return lax.ppermute(array, axis, pairs)


def causal_conv(rim_rows, inner_rows, weight, bias):
    length = inner_rows.shape[1]
    window = jnp.concatenate([rim_rows, inner_rows], axis=1)
    total = bias
    for tap_index in range(CONV):
        part = lax.slice_in_dim(window, tap_index, tap_index + length, axis=1)
        total = total + weight[tap_index].astype(jnp.float32) * part.astype(jnp.float32)
    return jax.nn.silu(total).astype(jnp.bfloat16)


def local(
    projected,
    state_maps,
    step_raw,
    step_bias,
    decay_rate,
    skip_gain,
    conv_weight,
    conv_bias,
    map_weight,
    map_bias,
):
    head_count = lax.axis_size("head")
    heads_here = step_bias.shape[0]
    seq_count = projected.shape[0]
    row_count = projected.shape[1]
    width = heads_here * HEAD_DIM
    repeats = head_count // GROUPS
    group_index = lax.axis_index("head") // repeats
    grouped = state_maps.reshape(seq_count, row_count, 2, GROUPS, STATE).transpose(0, 1, 3, 2, 4)
    spread = jnp.broadcast_to(
        grouped[:, :, :, None], (seq_count, row_count, GROUPS, repeats, 2, STATE)
    )
    sent_maps = spread.reshape(seq_count, row_count, head_count * 2 * STATE)
    local_x, local_step, local_maps = (
        lax.all_to_all(projected, "head", split_axis=2, concat_axis=1, tiled=True),
        lax.all_to_all(step_raw, "head", split_axis=2, concat_axis=1, tiled=True),
        lax.all_to_all(sent_maps, "head", split_axis=2, concat_axis=1, tiled=True),
    )
    length = local_x.shape[1]
    map_taps = lax.dynamic_slice_in_dim(
        map_weight.reshape(CONV, 2, GROUPS, STATE), group_index, 1, 2
    ).reshape(CONV, 2 * STATE)
    map_shift = lax.dynamic_slice_in_dim(
        map_bias.reshape(2, GROUPS, STATE), group_index, 1, 1
    ).reshape(2 * STATE)
    rim_x, rim_maps = from_behind(
        (local_x[:, length - CONV + 1 :], local_maps[:, length - CONV + 1 :]), "seq", 1
    )
    inner_x = causal_conv(rim_x, local_x, conv_weight, conv_bias)
    inner_maps = causal_conv(rim_maps, local_maps, map_taps, map_shift)
    delta = jax.nn.softplus(local_step.astype(jnp.float32) + step_bias)
    log_decay = -delta * decay_rate
    span_count = length // SPAN
    x_spans = inner_x.reshape(seq_count, span_count, SPAN, heads_here, HEAD_DIM)
    b_spans = inner_maps[:, :, :STATE].reshape(seq_count, span_count, SPAN, STATE)
    c_spans = inner_maps[:, :, STATE:].reshape(seq_count, span_count, SPAN, STATE)
    delta_spans = delta.reshape(seq_count, span_count, SPAN, heads_here)
    cumulative = jnp.cumsum(log_decay.reshape(seq_count, span_count, SPAN, heads_here), axis=2)
    lower = lax.broadcasted_iota(jnp.int32, (SPAN, SPAN), 0) >= lax.broadcasted_iota(
        jnp.int32, (SPAN, SPAN), 1
    )

    def span_work(index):
        x_here = lax.dynamic_index_in_dim(x_spans, index, 1, keepdims=False)
        b_here = lax.dynamic_index_in_dim(b_spans, index, 1, keepdims=False)
        c_here = lax.dynamic_index_in_dim(c_spans, index, 1, keepdims=False)
        delta_here = lax.dynamic_index_in_dim(delta_spans, index, 1, keepdims=False)
        cum_here = lax.dynamic_index_in_dim(cumulative, index, 1, keepdims=False)
        scores = jnp.einsum("stn,skn->stk", c_here, b_here, preferred_element_type=jnp.float32)
        cum_heads = cum_here.transpose(0, 2, 1)
        differ = cum_heads[:, :, :, None] - cum_heads[:, :, None, :]
        decay = jnp.where(lower, jnp.exp(jnp.minimum(differ, 0.0)), 0.0)
        weights = (scores[:, None] * decay * delta_here.transpose(0, 2, 1)[:, :, None, :]).astype(
            jnp.bfloat16
        )
        intra = jnp.einsum("shtk,skhp->sthp", weights, x_here, preferred_element_type=jnp.float32)
        scale = jnp.exp(cum_here[:, -1:] - cum_here) * delta_here
        carried = (x_here * scale[..., None]).astype(jnp.bfloat16)
        produced = jnp.einsum("skhp,skn->shpn", carried, b_here, preferred_element_type=jnp.float32)
        return (intra, produced)

    intra_all, produced_all = lax.map(span_work, jnp.arange(span_count, dtype=jnp.int32))
    totals = cumulative[:, :, -1]
    totals_first = jnp.moveaxis(totals, 1, 0)

    def advance(state_now, item):
        decay_total, produced = item
        return (jnp.exp(decay_total)[..., None, None] * state_now + produced, state_now)

    zero_state = jnp.zeros((seq_count, heads_here, HEAD_DIM, STATE), jnp.float32)
    block_end, entering_local = lax.scan(advance, zero_state, (totals_first, produced_all))
    block_total = jnp.sum(totals, axis=1)
    before_span = jnp.cumsum(totals, axis=1) - totals
    growth = jnp.exp(block_total)[..., None, None]

    def relay(turn, carried_pair):
        incoming = from_behind(carried_pair[1], "seq", 1)
        return (incoming, growth * incoming + block_end)

    incoming_state, _ = lax.fori_loop(0, lax.axis_size("seq") - 1, relay, (zero_state, block_end))
    entering = (
        entering_local
        + jnp.exp(jnp.moveaxis(before_span, 1, 0))[..., None, None] * incoming_state[None]
    )
    entering_b = entering.astype(jnp.bfloat16)
    inter = jnp.einsum("scqn,cshpn->scqhp", c_spans, entering_b, preferred_element_type=jnp.float32)
    intra = jnp.moveaxis(intra_all, 0, 1)
    mixed = (
        intra
        + jnp.exp(cumulative)[..., None] * inter
        + skip_gain[:, None] * x_spans.astype(jnp.float32)
    )
    mixed = mixed.astype(jnp.bfloat16).reshape(seq_count, length, width)
    return lax.all_to_all(mixed, "head", split_axis=1, concat_axis=2, tiled=True)


def solution(mesh):
    return jax.shard_map(
        local,
        mesh=mesh,
        in_specs=(
            P(None, ("seq", "head"), None),
            P(None, ("seq", "head"), None),
            P(None, ("seq", "head"), None),
            P("head"),
            P("head"),
            P("head"),
            P(None, "head"),
            P("head"),
            P(),
            P(),
        ),
        out_specs=P(None, ("seq", "head"), None),
        check_vma=False,
    )
```

profile of v0, /device:TPU:1, one launch (start us, length us, event | category | flops | bytes accessed | tf_op | source)
XLA Modules:
  0.0 617.9 jit_solution(12799777800667414941)
XLA Ops:
  1.7 8.6 %all-to-all-start.2 = ((bf16[32,2,512]{2,1,0:T(2,128)(2,1)}), bf16[32,2,512]{2,1,0:T(2,128)(2,1)S(1)}, u32[]{:S(2)}, u32[]{:S(2)}) async-start(bf16[32,2,512]{2,1,0:T(2,128)(2,1)} %reshape.173), calls=%async_computation.2 | async-start | bytes 131072 | tf_op jit(solution)/shard_map/all_to_all | solution.py:55
  13.3 5.7 broadcast_in_dim.20
  18.9 13.9 %reshape.171 = bf16[32,2,32768]{2,1,0:T(2,128)(2,1)} reshape(bf16[16384,2,64]{2,1,0:T(2,128)(2,1)} %bitcast.187) | data formatting | bytes 8388608
  32.8 7.4 %all-to-all-start.1 = ((bf16[32,2,32768]{2,1,0:T(2,128)(2,1)}), bf16[32,2,32768]{2,1,0:T(2,128)(2,1)}, u32[]{:S(2)}, u32[]{:S(2)}) async-start(bf16[32,2,32768]{2,1,0:T(2,128)(2,1)} %reshape.171), calls=%async_computation.1 | async-start | bytes 8388608 | tf_op jit(solution)/shard_map/all_to_all | solution.py:56
  40.3 17.8 %copy.77 = bf16[2,64,16384]{1,0,2:T(2,128)(2,1)} copy(bf16[2,64,16384]{2,1,0:T(8,128)(2,1)} %param.16) | data formatting | bytes 8388608 | tf_op args[0]
  58.0 13.9 %reshape.169 = bf16[32,2,32768]{2,1,0:T(2,128)(2,1)} reshape(bf16[16384,2,64]{2,1,0:T(2,128)(2,1)} %bitcast.190) | data formatting | bytes 8388608
  72.0 20.5 %all-to-all-done.1 = bf16[32,2,32768]{2,1,0:T(2,128)(2,1)} async-done(((bf16[32,2,32768]{2,1,0:T(2,128)(2,1)}), bf16[32,2,32768]{2,1,0:T(2,128)(2,1)}, u32[]{:S(2)}, u32[]{:S(2)}) %all-to-all-start.1) | async-done | bytes 4194336 | tf_op jit(solution)/shard_map/all_to_all | solution.py:56
  92.5 7.2 %all-to-all-start = ((bf16[32,2,32768]{2,1,0:T(2,128)(2,1)}), bf16[32,2,32768]{2,1,0:T(2,128)(2,1)}, u32[]{:S(2)}, u32[]{:S(2)}) async-start(bf16[32,2,32768]{2,1,0:T(2,128)(2,1)} %reshape.169), calls=%async_computation | async-start | bytes 8388608 | tf_op jit(solution)/shard_map/all_to_all | solution.py:54
  100.4 9.0 %reduce-window.6 = f32[2,8,8,2,128]{4,2,3,1,0:T(8,128)S(1)} reduce-window(f32[2,8,8,2,128]{4,2,3,1,0:T(8,128)S(1)} %copy.86, f32[]{:T(128)} %constant.75.clone.1), window={size=1x1x1x1x128 pad=0_0x0_0x0_0x0_0x127_0}, to_apply=%region_0.1 | reduce-window | flops 4161536 | bytes 262148 | tf_op jit(solution)/shard_map/reduce-window
  110.3 13.7 %reshape.172 = bf16[16384,2,64]{2,1,0:T(2,128)(2,1)} reshape(bf16[32,2,32768]{2,1,0:T(2,128)(2,1)} %all-to-all-done.1) | data formatting | bytes 8388608
  123.9 18.5 %copy.106 = bf16[2,64,32,512]{3,1,2,0:T(8,128)(2,1)} copy(bf16[2,64,32,512]{1,0,3,2:T(2,128)(2,1)} %bitcast.188) | data formatting | bytes 8388608 | tf_op jit(solution)/shard_map/all_to_all | solution.py:56
  146.7 5.1 all-to-all-done
  151.9 13.7 %reshape.170 = bf16[16384,2,64]{2,1,0:T(2,128)(2,1)} reshape(bf16[32,2,32768]{2,1,0:T(2,128)(2,1)} %all-to-all-done) | data formatting | bytes 8388608
  165.5 18.5 %copy.78 = bf16[2,64,32,512]{3,1,2,0:T(8,128)(2,1)} copy(bf16[2,64,32,512]{1,0,3,2:T(2,128)(2,1)} %bitcast.189) | data formatting | bytes 8388608 | tf_op jit(solution)/shard_map/all_to_all | solution.py:54
  184.7 3.7 collective-permute-start.1
  188.5 10.9 %multiply_convert_fusion.8 = bf16[2,2048,512]{2,1,0:T(8,128)(2,1)S(1)} fusion(bf16[2,2048,512]{2,1,0:T(8,128)(2,1)} %bitcast.192, bf16[2,3,512]{2,1,0:T(4,128)(2,1)S(1)} %collective-permute-done.2, f32[512]{0:T(512)S(1)} %bitcast.210, f32[512]{0:T(512)S(1)} %bitcast.208, f32[512]{0:T(512)S(1)} %bitcast.209, f32[512]{0:T(512)S(1)} %bitcast.207, ...), kind=kLoop, calls=%fused_computation.44 | loop fusion | flops 54525952 | bytes 8404992 | tf_op jit(solution)/shard_map/convert_element_type | solution.py:26
  201.7 7.0 %multiply_convert_fusion.9 = bf16[2,2048,512]{2,1,0:T(8,128)(2,1)} fusion(bf16[2,2048,512]{2,1,0:T(8,128)(2,1)S(1)} %bitcast.194, bf16[2,3,512]{2,1,0:T(4,128)(2,1)S(1)} %collective-permute-done.1, f32[512]{0:T(512)S(1)} %bitcast.214, f32[512]{0:T(512)S(1)} %bitcast.215, f32[512]{0:T(512)S(1)} %bitcast.213, f32[512]{0:T(512)S(1)} %bitcast.212, ...), kind=kLoop, calls=%fused_computation.45 | loop fusion | flops 54525952 | bytes 8404992 | tf_op jit(solution)/shard_map/convert_element_type | solution.py:26
  208.8 6.3 %copy.79 = bf16[2,2048,512]{1,2,0:T(8,128)(2,1)} copy(bf16[2,2048,512]{2,1,0:T(8,128)(2,1)} %multiply_convert_fusion.9) | data formatting | bytes 8388608 | tf_op jit(solution)/shard_map/convert_element_type | solution.py:26
  215.0 3.7 copy.121
  222.1 4.3 broadcast.35.clone
  226.4 85.7 %while.39 = (s32[]{:T(128)}, f32[8,2,256,8,64]{2,4,3,0,1:T(8,128)}, f32[8,2,8,64,256]{4,3,2,1,0:T(8,128)}, s32[8]{0:T(128)S(1)}, bf16[2,8,256,8,64]{2,4,3,0,1:T(...) while((s32[]{:T(128)}, f32[8,2,256,8,64]{2,4,3,0,1:T(8,128)}, ...), condition=%wide.region_3.4_spmd.clone, body=%wide.region_2.3_spmd.clone.sunk | while | flops 342695936 | bytes 5459311 | solution.py:101
  241.6 3.5 fusion.55
  252.2 3.6 fusion.55
  262.9 3.6 fusion.55
  273.7 3.6 fusion.55
  284.4 3.6 fusion.55
  305.8 3.6 fusion.55
  312.1 4.3 broadcast.35
  316.4 20.5 %while.40 = (s32[]{:T(128)}, f32[2,8,64,256]{3,2,1,0:T(8,128)S(1)}, f32[8,2,8,64,256]{4,3,2,1,0:T(8,128)}, f32[8,2,8]{2,0,1:T(8,128)S(1)}, f32[8,2,8,64,256]{4,3,2,1,0:T(8,128)}, /*index=5*/s32[]{:T(128)}, s32[]{:T(128)}) while((s32[]{:T(128)}, f32[2,8,64,256]{3,2,1,0:T(8,128)S(1)}, f32[8,2,8,64,256]{4,3,2,1,0:T(8,128)}, ...), condition=%wide.region_5.6_spmd.clone, body=%wide.region_4.5_spmd.clone.sunk | while | flops 1048579 | bytes 5243808 | solution.py:110
  336.9 166.9 %while.38 = (s32[]{:T(128)}, f32[2,8,64,256]{3,2,1,0:T(8,128)}, f32[2,8,64,256]{3,2,1,0:T(8,128)S(1)}, f32[2,8,1,1]{1,0,3,2:T(2,128)S(1)}, f32[2,8,64,256]{3,2,1,0:T(8,128)S(1)}, /*index=5*/s32[]{:T(128)}) while((s32[]{:T(128)}, f32[2,8,64,256]{3,2,1,0:T(8,128)}, f32[2,8,64,256]{3,2,1,0:T(8,128)S(1)}, f32[2,8,1,1]{1,0,3,2:T(2,128)S(1)}, ...), condition=%wide.region_9.10_spmd, body=%wide.region_8.9_spmd.sunk | while | flops 524290 | bytes 11534537 | solution.py:119
  337.0 3.6 collective-permute-start
  340.6 21.2 %collective-permute-done = f32[2,8,64,256]{3,2,1,0:T(8,128)S(1)} collective-permute-done((f32[2,8,64,256]{3,2,1,0:T(8,128)S(1)}, f32[2,8,64,256]{3,2,1,0:T(8,128)S(1)}, u32[]{:S(2)}, u32[]{:S(2)}) %collective-permute-start) | collective-permute-done | bytes 1048608 | tf_op jit(solution)/shard_map/while/body/eval_jaxpr/ppermute | solution.py:16
  362.8 4.2 collective-permute-start
  367.0 20.3 %collective-permute-done = f32[2,8,64,256]{3,2,1,0:T(8,128)S(1)} collective-permute-done((f32[2,8,64,256]{3,2,1,0:T(8,128)S(1)}, f32[2,8,64,256]{3,2,1,0:T(8,128)S(1)}, u32[]{:S(2)}, u32[]{:S(2)}) %collective-permute-start) | collective-permute-done | bytes 1048608 | tf_op jit(solution)/shard_map/while/body/eval_jaxpr/ppermute | solution.py:16
  388.2 4.2 collective-permute-start
  392.4 19.4 %collective-permute-done = f32[2,8,64,256]{3,2,1,0:T(8,128)S(1)} collective-permute-done((f32[2,8,64,256]{3,2,1,0:T(8,128)S(1)}, f32[2,8,64,256]{3,2,1,0:T(8,128)S(1)}, u32[]{:S(2)}, u32[]{:S(2)}) %collective-permute-start) | collective-permute-done | bytes 1048608 | tf_op jit(solution)/shard_map/while/body/eval_jaxpr/ppermute | solution.py:16
  412.8 4.2 collective-permute-start
  417.0 18.4 %collective-permute-done = f32[2,8,64,256]{3,2,1,0:T(8,128)S(1)} collective-permute-done((f32[2,8,64,256]{3,2,1,0:T(8,128)S(1)}, f32[2,8,64,256]{3,2,1,0:T(8,128)S(1)}, u32[]{:S(2)}, u32[]{:S(2)}) %collective-permute-start) | collective-permute-done | bytes 1048608 | tf_op jit(solution)/shard_map/while/body/eval_jaxpr/ppermute | solution.py:16
  436.4 4.2 collective-permute-start
  440.6 17.5 %collective-permute-done = f32[2,8,64,256]{3,2,1,0:T(8,128)S(1)} collective-permute-done((f32[2,8,64,256]{3,2,1,0:T(8,128)S(1)}, f32[2,8,64,256]{3,2,1,0:T(8,128)S(1)}, u32[]{:S(2)}, u32[]{:S(2)}) %collective-permute-start) | collective-permute-done | bytes 1048608 | tf_op jit(solution)/shard_map/while/body/eval_jaxpr/ppermute | solution.py:16
  459.1 5.1 collective-permute-start
  464.2 16.6 %collective-permute-done = f32[2,8,64,256]{3,2,1,0:T(8,128)S(1)} collective-permute-done((f32[2,8,64,256]{3,2,1,0:T(8,128)S(1)}, f32[2,8,64,256]{3,2,1,0:T(8,128)S(1)}, u32[]{:S(2)}, u32[]{:S(2)}) %collective-permute-start) | collective-permute-done | bytes 1048608 | tf_op jit(solution)/shard_map/while/body/eval_jaxpr/ppermute | solution.py:16
  481.8 5.4 collective-permute-start
  487.1 15.7 %collective-permute-done = f32[2,8,64,256]{3,2,1,0:T(8,128)S(1)} collective-permute-done((f32[2,8,64,256]{3,2,1,0:T(8,128)S(1)}, f32[2,8,64,256]{3,2,1,0:T(8,128)S(1)}, u32[]{:S(2)}, u32[]{:S(2)}) %collective-permute-start) | collective-permute-done | bytes 1048608 | tf_op jit(solution)/shard_map/while/body/eval_jaxpr/ppermute | solution.py:16
  503.8 11.4 %fusion.29 = bf16[2,8,256,8,64]{2,4,3,1,0:T(8,128)(2,1)} fusion(f32[8,2,256,8,64]{2,4,3,0,1:T(8,128)} %get-tuple-element.112, bf16[2,8,256,8,64]{2,1,4,3,0:T(8,128)(2,1)} %bitcast.186, f32[8]{0:T(128)S(1)} %copy-done.7, f32[2,8,256,8]{2,3,1,0:T(8,128)S(1)} %get-tuple-element.251, bf16[2,8,256,256,1]{3,2,4,1,0:T(8,128)(2,1)} %bitcast.33, ...), kind=kOutput, calls=%fused_computation.42 | convolution fusion | flops 1092616192 | bytes 28443168 | tf_op jit(solution)/shard_map/scqn,cshpn->scqhp/dot_general | solution.py:125
  515.2 10.9 %copy.107 = bf16[2,8,256,8,64]{4,3,0,2,1:T(8,128)(2,1)} copy(bf16[2,8,256,8,64]{2,4,3,1,0:T(8,128)(2,1)} %fusion.29) | data formatting | bytes 8388608 | tf_op jit(solution)/shard_map/reshape | solution.py:132
  526.1 13.1 %reshape.167 = bf16[2,2048,512]{2,0,1:T(2,128)(2,1)} reshape(bf16[2,8,256,8,64]{4,3,0,2,1:T(8,128)(2,1)} %copy.107) | data formatting | bytes 8388608 | tf_op jit(solution)/shard_map/reshape | solution.py:132
  539.2 75.6 %all_to_all.63 = bf16[2,2048,512]{2,0,1:T(2,128)(2,1)S(1)} all-to-all(bf16[2,2048,512]{2,0,1:T(2,128)(2,1)} %reshape.167), channel_id=1, replica_groups=mesh['seq'=8,'head'=32] {'head'}, dimensions={1} | all-to-all | bytes 8388608 | tf_op jit(solution)/shard_map/all_to_all | solution.py:133
  (218 shorter events, 96.1 us)
Async XLA Ops:
  1.7 31.1 %all-to-all-start.2 = ((bf16[32,2,512]{2,1,0:T(2,128)(2,1)}), bf16[32,2,512]{2,1,0:T(2,128)(2,1)S(1)}, u32[]{:S(2)}, u32[]{:S(2)}) async-start(bf16[32,2,512]{2,1,0:T(2,128)(2,1)} %reshape.173), calls=%async_computation.2 | async-start | bytes 131072 | tf_op jit(solution)/shard_map/all_to_all | solution.py:55
  32.8 59.7 %all-to-all-start.1 = ((bf16[32,2,32768]{2,1,0:T(2,128)(2,1)}), bf16[32,2,32768]{2,1,0:T(2,128)(2,1)}, u32[]{:S(2)}, u32[]{:S(2)}) async-start(bf16[32,2,32768]{2,1,0:T(2,128)(2,1)} %reshape.171), calls=%async_computation.1 | async-start | bytes 8388608 | tf_op jit(solution)/shard_map/all_to_all | solution.py:56
  58.0 41.7 %copy-start.3 = (bf16[4,4096]{1,0:T(4,128)(2,1)S(1)}, bf16[4,4096]{1,0:T(4,128)(2,1)}, u32[]{:S(2)}) copy-start(bf16[4,4096]{1,0:T(4,128)(2,1)} %param.24) | copy-start | bytes 98308
  58.0 41.7 %copy-start.4 = (f32[4096]{0:T(1024)S(1)}, f32[4096]{0:T(1024)}, u32[]{:S(2)}) copy-start(f32[4096]{0:T(1024)} %param.25) | copy-start | bytes 49156
  58.0 41.8 %copy-start.5 = (bf16[4,512]{1,0:T(4,128)(2,1)S(1)}, bf16[4,512]{1,0:T(4,128)(2,1)}, u32[]{:S(2)}) copy-start(bf16[4,512]{1,0:T(4,128)(2,1)} %param.22) | copy-start | bytes 12292
  58.0 42.2 %copy-start.8 = (f32[8]{0:T(128)S(1)}, f32[8]{0:T(128)}, u32[]{:S(2)}) copy-start(f32[8]{0:T(128)} %param.20) | copy-start | bytes 100
  58.0 42.2 %copy-start.9 = (f32[8]{0:T(128)S(1)}, f32[8]{0:T(128)}, u32[]{:S(2)}) copy-start(f32[8]{0:T(128)} %param.19) | copy-start | bytes 100
  92.5 59.4 %all-to-all-start = ((bf16[32,2,32768]{2,1,0:T(2,128)(2,1)}), bf16[32,2,32768]{2,1,0:T(2,128)(2,1)}, u32[]{:S(2)}, u32[]{:S(2)}) async-start(bf16[32,2,32768]{2,1,0:T(2,128)(2,1)} %reshape.169), calls=%async_computation | async-start | bytes 8388608 | tf_op jit(solution)/shard_map/all_to_all | solution.py:54
  143.2 45.3 %collective-permute-start.2 = (bf16[2,3,512]{2,1,0:T(4,128)(2,1)S(1)}, bf16[2,3,512]{2,1,0:T(4,128)(2,1)S(1)}, u32[]{:S(2)}, u32[]{:S(2)}) collective-permute-start(bf16[2,3,512]{2,1,0:T(4,128)(2,1)S(1)} %slice.98), channel_id=1, source_target_pairs={{0,32},{32,64},{64,96},{96,128},{128,160},{160,192},{192,224},{1,3... | collective-permute-start | bytes 18440 | tf_op jit(solution)/shard_map/ppermute | solution.py:16
  184.7 17.0 %collective-permute-start.1 = (bf16[2,3,512]{2,1,0:T(4,128)(2,1)S(1)}, bf16[2,3,512]{2,1,0:T(4,128)(2,1)S(1)}, u32[]{:S(2)}, u32[]{:S(2)}) collective-permute-start(bf16[2,3,512]{2,1,0:T(4,128)(2,1)S(1)} %slice.93), channel_id=1, source_target_pairs={{0,32},{32,64},{64,96},{96,128},{128,160},{160,192},{192,224},{1,3... | collective-permute-start | bytes 18440 | tf_op jit(solution)/shard_map/ppermute | solution.py:16
  188.5 13.2 %copy-start.2 = (bf16[2,64,32,512]{3,1,2,0:T(8,128)(2,1)S(1)}, bf16[2,64,32,512]{3,1,2,0:T(8,128)(2,1)}, u32[]{:S(2)}) copy-start(bf16[2,64,32,512]{3,1,2,0:T(8,128)(2,1)} %copy.78) | copy-start | bytes 12582916
  188.5 13.2 %copy-start.6 = (f32[512]{0:T(512)S(1)}, f32[512]{0:T(512)}, u32[]{:S(2)}) copy-start(f32[512]{0:T(512)} %param.23) | copy-start | bytes 6148
  218.7 7.7 %copy-start = (bf16[128,8,8,256]{3,2,1,0:T(8,128)(2,1)}, bf16[128,8,8,256]{3,2,1,0:T(8,128)(2,1)S(1)}, u32[]{:S(2)}) copy-start(bf16[128,8,8,256]{3,2,1,0:T(8,128)(2,1)S(1)} %copy.121) | copy-start | bytes 12582916
  336.9 166.9 %copy-start.7 = (f32[8]{0:T(128)S(1)}, f32[8]{0:T(128)}, u32[]{:S(2)}) copy-start(f32[8]{0:T(128)} %param.21) | copy-start | bytes 100
  337.0 24.9 %collective-permute-start = (f32[2,8,64,256]{3,2,1,0:T(8,128)S(1)}, f32[2,8,64,256]{3,2,1,0:T(8,128)S(1)}, u32[]{:S(2)}, u32[]{:S(2)}) collective-permute-start(f32[2,8,64,256]{3,2,1,0:T(8,128)S(1)} %get-tuple-element.445), channel_id=1, source_target_pairs={{0,32},{32,64},{64,96},{96,128},{128,160},{160,192},{192,224},{1,3... | collective-permute-start | bytes 3145736 | tf_op jit(solution)/shard_map/while/body/eval_jaxpr/ppermute | solution.py:16
  361.8 1.0 copy-start.1
  362.8 24.5 %collective-permute-start = (f32[2,8,64,256]{3,2,1,0:T(8,128)S(1)}, f32[2,8,64,256]{3,2,1,0:T(8,128)S(1)}, u32[]{:S(2)}, u32[]{:S(2)}) collective-permute-start(f32[2,8,64,256]{3,2,1,0:T(8,128)S(1)} %get-tuple-element.445), channel_id=1, source_target_pairs={{0,32},{32,64},{64,96},{96,128},{128,160},{160,192},{192,224},{1,3... | collective-permute-start | bytes 3145736 | tf_op jit(solution)/shard_map/while/body/eval_jaxpr/ppermute | solution.py:16
  387.3 1.0 copy-start.1
  388.2 23.6 %collective-permute-start = (f32[2,8,64,256]{3,2,1,0:T(8,128)S(1)}, f32[2,8,64,256]{3,2,1,0:T(8,128)S(1)}, u32[]{:S(2)}, u32[]{:S(2)}) collective-permute-start(f32[2,8,64,256]{3,2,1,0:T(8,128)S(1)} %get-tuple-element.445), channel_id=1, source_target_pairs={{0,32},{32,64},{64,96},{96,128},{128,160},{160,192},{192,224},{1,3... | collective-permute-start | bytes 3145736 | tf_op jit(solution)/shard_map/while/body/eval_jaxpr/ppermute | solution.py:16
  411.8 1.0 copy-start.1
  412.8 22.6 %collective-permute-start = (f32[2,8,64,256]{3,2,1,0:T(8,128)S(1)}, f32[2,8,64,256]{3,2,1,0:T(8,128)S(1)}, u32[]{:S(2)}, u32[]{:S(2)}) collective-permute-start(f32[2,8,64,256]{3,2,1,0:T(8,128)S(1)} %get-tuple-element.445), channel_id=1, source_target_pairs={{0,32},{32,64},{64,96},{96,128},{128,160},{160,192},{192,224},{1,3... | collective-permute-start | bytes 3145736 | tf_op jit(solution)/shard_map/while/body/eval_jaxpr/ppermute | solution.py:16
  435.4 1.0 copy-start.1
  436.4 21.7 %collective-permute-start = (f32[2,8,64,256]{3,2,1,0:T(8,128)S(1)}, f32[2,8,64,256]{3,2,1,0:T(8,128)S(1)}, u32[]{:S(2)}, u32[]{:S(2)}) collective-permute-start(f32[2,8,64,256]{3,2,1,0:T(8,128)S(1)} %get-tuple-element.445), channel_id=1, source_target_pairs={{0,32},{32,64},{64,96},{96,128},{128,160},{160,192},{192,224},{1,3... | collective-permute-start | bytes 3145736 | tf_op jit(solution)/shard_map/while/body/eval_jaxpr/ppermute | solution.py:16
  458.1 1.0 copy-start.1
  459.1 21.7 %collective-permute-start = (f32[2,8,64,256]{3,2,1,0:T(8,128)S(1)}, f32[2,8,64,256]{3,2,1,0:T(8,128)S(1)}, u32[]{:S(2)}, u32[]{:S(2)}) collective-permute-start(f32[2,8,64,256]{3,2,1,0:T(8,128)S(1)} %get-tuple-element.445), channel_id=1, source_target_pairs={{0,32},{32,64},{64,96},{96,128},{128,160},{160,192},{192,224},{1,3... | collective-permute-start | bytes 3145736 | tf_op jit(solution)/shard_map/while/body/eval_jaxpr/ppermute | solution.py:16
  480.8 1.0 copy-start.1
  481.8 21.1 %collective-permute-start = (f32[2,8,64,256]{3,2,1,0:T(8,128)S(1)}, f32[2,8,64,256]{3,2,1,0:T(8,128)S(1)}, u32[]{:S(2)}, u32[]{:S(2)}) collective-permute-start(f32[2,8,64,256]{3,2,1,0:T(8,128)S(1)} %get-tuple-element.445), channel_id=1, source_target_pairs={{0,32},{32,64},{64,96},{96,128},{128,160},{160,192},{192,224},{1,3... | collective-permute-start | bytes 3145736 | tf_op jit(solution)/shard_map/while/body/eval_jaxpr/ppermute | solution.py:16
  502.8 1.0 copy-start.1
where the time goes:
time: 628 us; the launch traced here: 618 us
  local copies, waits for them, and re-layouts  190 us (30%)
  waiting for transfers between devices  155 us (25%)
  blocking collectives  75.6 us (12%)
  matrix products  69.6 us (11%)
  starting transfers between devices  61.2 us (10%)
  other arithmetic  50.7 us (8%)
  loops' own time  15.6 us (2%)
    ppermute x9, waiting for transfers between devices, from_behind(): return lax.ppermute(array, axis, pairs)  129 us
    unnamed x31, local copies, waits for them, and re-layouts  83.4 us
    all_to_all x1, blocking collectives, local(): lax.all_to_all(mixed, 'head', split_axis=1, concat_axis=2, tiled=True)  75.6 us
    ppermute x9, starting transfers between devices, from_behind(): return lax.ppermute(array, axis, pairs)  38 us
    dot_general x8, matrix products, span_work(): jnp.einsum('shtk,skhp->sthp', weights, x_here, preferred_element_type=jnp...  28.4 us
    reshape x2, local copies, waits for them, and re-layouts, local(): mixed = mixed.astype(jnp.bfloat16).reshape(seq_count, length, width)  24 us
    all_to_all x1, waiting for transfers between devices, local(): lax.all_to_all(sent_maps, 'head', split_axis=2, concat_axis=1, tiled=True)  20.5 us
    dot_general x8, matrix products, span_work(): jnp.einsum('skhp,skn->shpn', carried, b_here, preferred_element_type=jnp....  19.4 us
  transfers between devices with their start and end apart: 12, of which 9 were waited for; matrix products, arithmetic and copies ran while one was open for 23% of the time, Pallas kernels for 0%

commit v1 on v0

v1 whole, which is shorter than its diff:
```python
import jax
import jax.numpy as jnp
from jax import lax
from jax.experimental import pallas as pl
from jax.experimental.pallas import tpu as pltpu
from jax.sharding import PartitionSpec as P

MESH = pl.DeviceIdType.MESH
F32 = jnp.float32
BF16 = jnp.bfloat16
SPAN = 256
TOK = 64
LEN = 2048
SPANS = LEN // SPAN
NHEAD = 32
NSEQ = 8
BATCH = 4
CH = 256
EDGE = 16
DI = 16384
LOG2E = 1.4426950408889634
CAP = 64.0


def dot(a, b):
    return jnp.dot(a, b, preferred_element_type=F32)


def split(v):
    high = v.astype(BF16).astype(F32)
    rest = v - high
    middle = rest.astype(BF16).astype(F32)
    return high, middle, rest - middle


def silu(v):
    return v / (1.0 + jnp.exp(-v))


def kernel(
    proj, maps, step, sb, dr, sg, cw, cb, mw, mb, out,
    xin, mapin, mapc, bt, sc, xi, hs, hc, intra, ob, win, stt, stin, stf, pk, pkall,
    cumr, delr, work, rs, b2, zs1, zr1, zs2, hin, wrow,
    rx, rhx, rz1, rz2, rmap, rstep, rpar, rhm, rsib, rout,
    sx, smap, sstep, spar, shx, shm, ssib, sz1, sz2, sout,
):
    h = lax.axis_index("head")
    z = lax.axis_index("seq")
    g = h // 4
    r = lax.rem(h, 4)
    c = lax.rem(h, 2)
    seq = r // 2
    hb = g * 2 + c

    def peer(i):
        return lax.rem(h + i, NHEAD)

    def zpeer(i):
        return lax.rem(z + i, NSEQ)

    barrier = pltpu.get_barrier_semaphore()

    def greet(i, carry):
        pl.semaphore_signal(barrier, 1, device_id=(z, peer(i)), device_id_type=MESH)
        return carry

    def greet_z(i, carry):
        pl.semaphore_signal(barrier, 1, device_id=(zpeer(i), h), device_id_type=MESH)
        return carry

    lax.fori_loop(1, NHEAD, greet, 0)
    lax.fori_loop(1, NSEQ, greet_z, 0)
    pl.semaphore_wait(barrier, NHEAD - 1 + NSEQ - 1)

    def cols(start, width=CH):
        return pl.ds(pl.multiple_of(start, 128), width)

    def rows(start, count):
        return pl.ds(pl.multiple_of(start, 16), count)

    def map_src(d):
        return maps.at[lax.rem(d // 2, 2), :, cols(lax.rem(d, 2) * 2048 + (d // 4) * 256)]

    def x_src(d, b):
        base = ((d // 4) * 2 + lax.rem(d, 2)) * 1024
        return proj.at[lax.rem(d // 2, 2), :, cols(base + b * CH)]

    def st_src(d):
        return stt.at[lax.rem(d // 2, 2), rows(((d // 4) * 2 + lax.rem(d, 2)) * 16, 16), :]

    map_dst = mapin.at[rows(EDGE + h * TOK, TOK), :]

    def send_map(i, carry):
        d = peer(i)
        pltpu.make_async_remote_copy(
            map_src(d), map_dst, smap, rmap, device_id=(z, d), device_id_type=MESH
        ).start()
        return carry

    def send_x(b):
        dst = xin.at[b, rows(EDGE + h * TOK, TOK), :]
        pltpu.make_async_copy(x_src(h, b), dst, rx.at[b]).start()

        def one(i, carry):
            d = peer(i)
            pltpu.make_async_remote_copy(
                x_src(d, b), dst, sx, rx.at[b], device_id=(z, d), device_id_type=MESH
            ).start()
            return carry

        lax.fori_loop(1, NHEAD, one, 0)

    pltpu.make_async_copy(map_src(h), map_dst, rmap).start()
    lax.fori_loop(1, NHEAD, send_map, 0)
    send_x(0)

    eye = lax.broadcasted_iota(jnp.int32, (8, 8), 0) == lax.broadcasted_iota(jnp.int32, (8, 8), 1)

    def column(ref):
        return jnp.sum(jnp.where(eye, jnp.broadcast_to(ref[...], (8, 8)), 0.0), axis=1, keepdims=True)

    owner = lax.broadcasted_iota(jnp.int32, (8, 512), 1) // 64 == lax.broadcasted_iota(
        jnp.int32, (8, 512), 0
    )
    pk[0:4, 0:512] = cw[...].astype(F32)
    pk[4:5, 0:512] = cb[...]
    pk[5:6, 0:512] = jnp.sum(jnp.where(owner, column(sg), 0.0), axis=0, keepdims=True)
    pk[6:8, 0:512] = jnp.zeros((2, 512), F32)
    pk[:, 512:640] = jnp.broadcast_to(column(sb), (8, 128))
    pk[:, 640:768] = jnp.broadcast_to(column(dr), (8, 128))
    pltpu.make_async_copy(pk, pkall.at[r], rpar).start()
    for i in range(1, 4):
        pltpu.make_async_remote_copy(
            pk, pkall.at[r], spar, rpar, device_id=(z, g * 4 + lax.rem(r + i, 4)), device_id_type=MESH
        ).start()

    half = lax.broadcasted_iota(jnp.int32, (2 * TOK, 256), 0) // TOK == c
    for s in range(2):
        v = step[s].astype(F32)
        v = jnp.where(half, jnp.concatenate([v, v], axis=0), 0.0)
        stt[s] = v.T.astype(BF16)
    pltpu.make_async_copy(st_src(h), stin.at[h], rstep).start()

    def send_step(i, carry):
        d = peer(i)
        pltpu.make_async_remote_copy(
            st_src(d), stin.at[h], sstep, rstep, device_id=(z, d), device_id_type=MESH
        ).start()
        return carry

    lax.fori_loop(1, NHEAD, send_step, 0)
    send_x(1)

    def done(ref, sem):
        pltpu.make_async_copy(ref, ref, sem).wait()

    def conv(src, k, weight, bias, store):
        def part(i, carry):
            start = pl.multiple_of(k * SPAN + i * 64, 16)
            for j in range(2):
                lanes = slice(j * 128, (j + 1) * 128)
                win[j] = src[pl.ds(start, 64 + EDGE), lanes].astype(F32)
                total = bias[:, lanes]
                for tap in range(4):
                    total = total + weight[tap : tap + 1, lanes] * win[j, 13 + tap : 77 + tap, :]
                store(start, lanes, silu(total).astype(BF16))
            return carry

        lax.fori_loop(0, SPAN // 64, part, 0)

    def edge(buffer, send_sem, recv_sem):
        return pltpu.make_async_remote_copy(
            buffer.at[pl.ds(LEN, EDGE), :], buffer.at[pl.ds(0, EDGE), :],
            send_sem, recv_sem, device_id=(zpeer(1), h), device_id_type=MESH,
        )

    def first_block(buffer):
        @pl.when(z == 0)
        def _():
            buffer[0:EDGE, :] = jnp.zeros((EDGE, CH), BF16)

    done(pkall, rpar)
    done(stin, rstep)
    for i in range(16):
        stf[:, i * 128 : (i + 1) * 128] = stin[2 * i].astype(F32) + stin[2 * i + 1].astype(F32)
    bias_col = jnp.concatenate([pkall[2 * c, :, 512:513], pkall[2 * c + 1, :, 512:513]], axis=0)
    rate_col = jnp.concatenate([pkall[2 * c, :, 640:641], pkall[2 * c + 1, :, 640:641]], axis=0)
    upper = (
        lax.broadcasted_iota(jnp.int32, (SPAN, SPAN), 0)
        <= lax.broadcasted_iota(jnp.int32, (SPAN, SPAN), 1)
    ).astype(BF16)
    for k in range(SPANS):
        v = stf[:, k * SPAN : (k + 1) * SPAN] + bias_col
        delta = jnp.maximum(v, 0.0) + jnp.log1p(jnp.exp(-jnp.abs(v)))
        delr[k] = delta
        first, second, third = split(-delta * rate_col * LOG2E)
        cumr[k] = (
            dot(first.astype(BF16), upper) + dot(second.astype(BF16), upper)
        ) + dot(third.astype(BF16), upper)

    def rows_of(k, carry):
        cum = cumr[k]
        delta = delr[k]
        scale = jnp.exp2(cum[:, SPAN - 1 :] - cum) * delta
        s_high, s_low, _ = split(scale)
        e_high, e_mid, e_low = split(jnp.exp2(cum))
        work[0] = cum
        work[1] = s_high
        work[2] = s_low
        work[3] = e_high
        work[4] = e_mid
        work[5] = e_low
        work[6] = jnp.log(delta) * LOG2E - cum
        blank = jnp.zeros((4, SPAN), F32)
        for b in range(BATCH):
            at = slice(4 * b, 4 * b + 4)
            rs[k, b, 0:4] = work[0, at]
            rs[k, b, 4:8] = blank
            rs[k, b, 8:12] = work[1, at]
            rs[k, b, 12:16] = work[2, at]
            rs[k, b, 16:20] = work[3, at]
            rs[k, b, 20:24] = work[4, at]
            rs[k, b, 24:28] = work[5, at]
            rs[k, b, 28:32] = blank
            b2[k, b, 0:4] = work[6, at]
            b2[k, b, 4:8] = blank
        return carry

    lax.fori_loop(0, SPANS, rows_of, 0)
    send_x(2)

    done(mapin.at[pl.ds(EDGE, LEN), :], rmap)
    edge(mapin, shm, rhm).start()
    done(mapin.at[pl.ds(0, EDGE), :], rhm)
    first_block(mapin)
    which = cols(c * 2048 + g * 256)
    map_weight = mw[:, which].astype(F32)
    map_bias = mb[:, which]

    def map_span(k, carry):
        def store(start, lanes, value):
            mapc[c, pl.ds(start, 64), lanes] = value

        conv(mapin, k, map_weight, map_bias, store)
        return carry

    lax.fori_loop(0, SPANS, map_span, 0)
    pltpu.make_async_remote_copy(
        mapc.at[c], mapc.at[c], ssib, rsib, device_id=(z, g * 4 + seq * 2 + 1 - c), device_id_type=MESH
    ).start()
    done(mapc.at[1 - c], rsib)
    send_x(3)

    causal = lax.broadcasted_iota(jnp.int32, (SPAN, SPAN), 0) >= lax.broadcasted_iota(
        jnp.int32, (SPAN, SPAN), 1
    )

    def scores(k, carry):
        at = pl.ds(pl.multiple_of(k * SPAN, SPAN), SPAN)
        bt[k] = mapc[0, at, :].astype(F32).T.astype(BF16)
        sc[k] = jnp.where(causal, dot(mapc[1, at, :], bt[k]), 0.0)
        return carry

    lax.fori_loop(0, SPANS, scores, 0)

    row_id = lax.broadcasted_iota(jnp.int32, (32, CH), 0)
    same = lax.rem(row_id, 4) == lax.broadcasted_iota(jnp.int32, (32, CH), 1) // 64
    pick_scale = (same & (row_id >= 8) & (row_id < 16)).astype(BF16)
    pick_decay = (same & (row_id >= 16) & (row_id < 28)).astype(BF16)
    low_lanes = lax.broadcasted_iota(jnp.int32, (SPAN, 128), 1) < 64

    def params_of(b):
        return pkall.at[2 * c + b // 2, :, cols(lax.rem(b, 2) * CH)]

    def states(b):
        two = lax.rem(b, 2)
        done(xin.at[b, pl.ds(EDGE, LEN), :], rx.at[b])
        edge(xin.at[b], shx, rhx.at[b]).start()
        done(xin.at[b, pl.ds(0, EDGE), :], rhx.at[b])
        first_block(xin.at[b])
        par = params_of(b)
        weight = par[0:4, :]
        bias = par[4:5, :]
        hc[...] = jnp.zeros_like(hc)
        wrow[two, 0] = jnp.ones((8, CH), F32)

        def span(k, carry):
            def store(start, lanes, value):
                xi[two, pl.ds(start, 64), lanes] = value

            conv(xin.at[b], k, weight, bias, store)
            at = pl.ds(pl.multiple_of(k * SPAN, SPAN), SPAN)
            stack = rs[k, b].T.astype(BF16)
            scale = dot(stack, pick_scale)
            growth = dot(stack[SPAN - 16 :], pick_decay)[15:16]
            carried = (xi[two, at, :].astype(F32) * scale).astype(BF16)
            produced = dot(bt[k], carried)
            state = hc[...]
            hs[two, k] = state
            hc[...] = growth * state + produced
            wrow[two, k + 1] = wrow[two, k] * growth
            return carry

        lax.fori_loop(0, SPANS, span, 0)
        for j in range(NSEQ):
            zs1[b * NSEQ + j, 0:32, :] = hc[j * 32 : (j + 1) * 32, :]
            zs1[b * NSEQ + j, 32:40, :] = wrow[two, SPANS]
        pltpu.make_async_copy(zs1.at[b * NSEQ + z], zr1.at[b, z], rz1.at[b]).start()

        def send(i, carry):
            d = zpeer(i)
            pltpu.make_async_remote_copy(
                zs1.at[b * NSEQ + d], zr1.at[b, z], sz1, rz1.at[b], device_id=(d, h), device_id_type=MESH
            ).start()
            return carry

        lax.fori_loop(1, NSEQ, send, 0)

    def relay(b):
        done(zr1.at[b], rz1.at[b])
        state = jnp.zeros((32, CH), F32)
        for j in range(NSEQ):
            zs2[b * NSEQ + j] = state
            state = zr1[b, j, 32:33, :] * state + zr1[b, j, 0:32, :]
        here = hin.at[b, pl.ds(pl.multiple_of(z * 32, 32), 32), :]
        pltpu.make_async_copy(zs2.at[b * NSEQ + z], here, rz2.at[b]).start()

        def send(i, carry):
            d = zpeer(i)
            pltpu.make_async_remote_copy(
                zs2.at[b * NSEQ + d], here, sz2, rz2.at[b], device_id=(d, h), device_id_type=MESH
            ).start()
            return carry

        lax.fori_loop(1, NSEQ, send, 0)

    def within(b):
        two = lax.rem(b, 2)
        skip = params_of(b)[5:6, :]

        def span(k, carry):
            at = pl.ds(pl.multiple_of(k * SPAN, SPAN), SPAN)
            columns = rs[k, b, 0:8].T
            own = sc[k]
            for pair in range(2):
                lanes = slice(pair * 128, (pair + 1) * 128)
                x_pair = xi[two, at, lanes]
                sums = []
                for one in range(2):
                    i = pair * 2 + one
                    exponent = columns[:, i : i + 1] + b2[k, b, i : i + 1]
                    weights = (jnp.exp2(jnp.minimum(exponent, CAP)) * own).astype(BF16)
                    sums.append(dot(weights, x_pair))
                intra[two, at, lanes] = (
                    jnp.where(low_lanes, sums[0], sums[1]) + skip[:, lanes] * x_pair.astype(F32)
                )
            return carry

        lax.fori_loop(0, SPANS, span, 0)

    def finish(b):
        two = lax.rem(b, 2)
        done(hin.at[b], rz2.at[b])

        def span(i, carry):
            k = lax.rem(g + i, SPANS)
            at = pl.ds(pl.multiple_of(k * SPAN, SPAN), SPAN)
            entering = (hs[two, k] + wrow[two, k, 0:1] * hin[b]).astype(BF16)
            inter = dot(mapc[1, at, :], entering)
            decay = dot(rs[k, b].T.astype(BF16), pick_decay)
            ob[b, at, :] = (intra[two, at, :] + decay * inter).astype(BF16)
            for j in range(4):
                d = k * 4 + lax.rem(r + j, 4)
                src = ob.at[b, rows(d * TOK, TOK), :]
                dst = out.at[seq, :, cols(hb * 1024 + b * CH)]

                @pl.when(d == h)
                def _():
                    pltpu.make_async_copy(src, dst, rout).start()

                @pl.when(d != h)
                def _():
                    pltpu.make_async_remote_copy(
                        src, dst, sout, rout, device_id=(z, d), device_id_type=MESH
                    ).start()

            return carry

        lax.fori_loop(0, SPANS, span, 0)

    def turn(i, carry):
        @pl.when(i < BATCH)
        def _():
            states(i)

        @pl.when(i > 0)
        def _():
            relay(i - 1)

        @pl.when(i < BATCH)
        def _():
            within(i)

        @pl.when(i > 0)
        def _():
            finish(i - 1)

        return carry

    lax.fori_loop(0, BATCH + 1, turn, 0)

    most = DI - DI // NHEAD
    done(proj.at[:, :, pl.ds(0, most)], sx)
    done(mapin.at[pl.ds(0, LEN - TOK), :], smap)
    done(stin.at[pl.ds(0, NHEAD - 1)], sstep)
    done(pkall.at[pl.ds(0, 3)], spar)
    done(xin.at[0, pl.ds(0, BATCH * EDGE), :], shx)
    done(mapin.at[pl.ds(0, EDGE), :], shm)
    done(mapc.at[0], ssib)
    done(zs1.at[pl.ds(0, BATCH * (NSEQ - 1))], sz1)
    done(zs2.at[pl.ds(0, BATCH * (NSEQ - 1))], sz2)
    done(out.at[:, :, pl.ds(0, most)], sout)
    done(out, rout)


def local(proj, maps, step, sb, dr, sg, cw, cb, mw, mb):
    vmem = pl.BlockSpec(memory_space=pltpu.VMEM)
    hbm = pl.BlockSpec(memory_space=pl.ANY)
    dma = pltpu.SemaphoreType.DMA
    scratch = [
        pltpu.VMEM((BATCH, EDGE + LEN, CH), BF16),
        pltpu.VMEM((EDGE + LEN, CH), BF16),
        pltpu.VMEM((2, LEN, CH), BF16),
        pltpu.VMEM((SPANS, 256, SPAN), BF16),
        pltpu.VMEM((SPANS, SPAN, SPAN), F32),
        pltpu.VMEM((2, LEN, CH), BF16),
        pltpu.VMEM((2, SPANS, 256, CH), F32),
        pltpu.VMEM((256, CH), F32),
        pltpu.VMEM((2, LEN, CH), F32),
        pltpu.VMEM((BATCH, LEN, CH), BF16),
        pltpu.VMEM((2, 64 + EDGE, 128), F32),
        pltpu.VMEM((2, 256, 128), BF16),
        pltpu.VMEM((NHEAD, 16, 128), BF16),
        pltpu.VMEM((16, LEN), F32),
        pltpu.VMEM((8, 768), F32),
        pltpu.VMEM((4, 8, 768), F32),
        pltpu.VMEM((SPANS, 16, SPAN), F32),
        pltpu.VMEM((SPANS, 16, SPAN), F32),
        pltpu.VMEM((7, 16, SPAN), F32),
        pltpu.VMEM((SPANS, BATCH, 32, SPAN), F32),
        pltpu.VMEM((SPANS, BATCH, 8, SPAN), F32),
        pltpu.VMEM((BATCH * NSEQ, 40, CH), F32),
        pltpu.VMEM((BATCH, NSEQ, 40, CH), F32),
        pltpu.VMEM((BATCH * NSEQ, 32, CH), F32),
        pltpu.VMEM((BATCH, 256, CH), F32),
        pltpu.VMEM((2, SPANS + 1, 8, CH), F32),
    ]
    scratch += [dma((BATCH,))] * 4 + [dma] * 16
    return pl.pallas_call(
        kernel,
        out_shape=jax.ShapeDtypeStruct(proj.shape, BF16),
        in_specs=[hbm, hbm] + [vmem] * 8,
        out_specs=hbm,
        scratch_shapes=scratch,
        compiler_params=pltpu.CompilerParams(
            collective_id=0, has_side_effects=True, vmem_limit_bytes=48 * 1024 * 1024
        ),
    )(
        proj, maps, step, sb.reshape(1, -1), dr.reshape(1, -1), sg.reshape(1, -1),
        cw, cb.reshape(1, -1), mw, mb.reshape(1, -1),
    )


def solution(mesh):
    return jax.shard_map(
        local,
        mesh=mesh,
        in_specs=(
            P(None, ("seq", "head"), None),
            P(None, ("seq", "head"), None),
            P(None, ("seq", "head"), None),
            P("head"),
            P("head"),
            P("head"),
            P(None, "head"),
            P("head"),
            P(),
            P(),
        ),
        out_specs=P(None, ("seq", "head"), None),
        check_vma=False,
    )
```

time: 628 us -> 196 us (0.31)
  the two profiles are of different devices: /device:TPU:1 before, /device:TPU:93 now
where the time goes in v1:
time: 196 us; the launch traced here: 195 us
  Pallas kernels  186 us (95%)
  local copies, waits for them, and re-layouts  8.88 us (5%)
    pallas_call x1, Pallas kernels, local(): pl.pallas_call(kernel, out_shape=jax.ShapeDtypeStruct(proj.shape, BF16),...  186 us
    unnamed x19, local copies, waits for them, and re-layouts  8.88 us

profile of v1, /device:TPU:93, one launch (start us, length us, event | category | flops | bytes accessed | tf_op | source)
XLA Modules:
  0.0 195.2 jit_solution(12816446590337165001)
XLA Ops:
  0.0 0.0 copy-start
  0.0 1.2 copy-done
  1.2 0.0 copy-start.1
  1.2 0.8 copy-done.1
  2.1 0.0 copy-start.2
  2.1 0.8 copy-done.2
  2.8 0.0 copy-start.3
  2.8 0.7 copy-done.3
  3.5 0.0 copy-start.4
  3.5 0.7 copy-done.4
  4.2 0.0 copy-start.5
  4.2 0.7 copy-done.5
  4.9 0.0 copy-start.6
  4.9 0.7 copy-done.6
  5.6 0.0 copy-start.7
  5.6 0.7 copy-done.7
  6.2 0.0 copy-start.8
  6.2 0.7 copy-done.8
  6.9 186.3 %shard_map.100 = bf16[2,64,16384]{2,1,0:T(8,128)(2,1)S(1)} custom-call(bf16[2,64,16384]{2,1,0:T(8,128)(2,1)} %proj.1, bf16[2,64,4096]{2,1,0:T(8,128)(2,1)S(1)} %copy-done, bf16[2,64,256]{2,1,0:T(8,128)(2,1)S(1)} %copy-done.1, f32[1,8]{1,0:T(1,128)S(1)} %bitcast.7, f32[1,8]{1,0:T(1,128)S(1)} %bitcast.8, f32[1,8]{1,0:T(1,128)S(1)} %bitcast.9, ...), custom_call_target="tpu_custom_call" | custom-call | tf_op jit(solution)/shard_map/pallas_call | solution.py:459
  193.2 2.0 %copy.12 = bf16[2,64,16384]{2,1,0:T(8,128)(2,1)} copy(bf16[2,64,16384]{2,1,0:T(8,128)(2,1)S(1)} %shard_map.100) | data formatting | bytes 8388608
Async XLA Ops:
  0.0 1.2 copy-start
  1.2 0.8 copy-start.1
  2.1 0.8 copy-start.2
  2.8 0.7 copy-start.3
  3.5 0.7 copy-start.4
  4.2 0.7 copy-start.5
  4.9 0.7 copy-start.6
  5.6 0.7 copy-start.7
  6.2 0.7 copy-start.8

commit v2 on v1

--- a/solution.py
+++ b/solution.py
@@ -16,6 +16,7 @@
 NSEQ = 8
 BATCH = 4
 CH = 256
+STRIDE = 5
 EDGE = 16
 DI = 16384
 LOG2E = 1.4426950408889634
@@ -38,10 +39,11 @@
 
 
 def kernel(
-    proj, maps, step, sb, dr, sg, cw, cb, mw, mb, out,
-    xin, mapin, mapc, bt, sc, xi, hs, hc, intra, ob, win, stt, stin, stf, pk, pkall,
-    cumr, delr, work, rs, b2, zs1, zr1, zs2, hin, wrow,
-    rx, rhx, rz1, rz2, rmap, rstep, rpar, rhm, rsib, rout,
+    proj, maps, step_in, sb_in, dr_in, sg_in, cw_in, cb_in, mw_in, mb_in, out,
+    step, sb, dr, sg, cw, cb, mw, mb,
+    xin, mapin, mapc, bt, sc, xi, hs, intra, ob, win, stt, stin, stf, pk, pkall,
+    cumr, delr, work, rs, b2, zs1, zr1, zs2, hin, wrow, grow,
+    small, rx, rhx, rz1, rz2, rmap, rstep, rpar, rhm, rsib, rout,
     sx, smap, sstep, spar, shx, shm, ssib, sz1, sz2, sout,
 ):
     h = lax.axis_index("head")
@@ -53,7 +55,7 @@
     hb = g * 2 + c
 
     def peer(i):
-        return lax.rem(h + i, NHEAD)
+        return lax.rem(h + i * STRIDE, NHEAD)
 
     def zpeer(i):
         return lax.rem(z + i, NSEQ)
@@ -70,7 +72,17 @@
 
     lax.fori_loop(1, NHEAD, greet, 0)
     lax.fori_loop(1, NSEQ, greet_z, 0)
-    pl.semaphore_wait(barrier, NHEAD - 1 + NSEQ - 1)
+    arrivals = [
+        pltpu.make_async_copy(src, dst, small.at[i])
+        for i, (src, dst) in enumerate(
+            [(step_in, step), (sb_in, sb), (dr_in, dr), (sg_in, sg), (cw_in, cw), (cb_in, cb),
+             (mw_in, mw), (mb_in, mb)]
+        )
+    ]
+    for arrival in arrivals:
+        arrival.start()
+    for arrival in arrivals:
+        arrival.wait()
 
     def cols(start, width=CH):
         return pl.ds(pl.multiple_of(start, 128), width)
@@ -109,10 +121,6 @@
             return carry
 
         lax.fori_loop(1, NHEAD, one, 0)
-
-    pltpu.make_async_copy(map_src(h), map_dst, rmap).start()
-    lax.fori_loop(1, NHEAD, send_map, 0)
-    send_x(0)
 
     eye = lax.broadcasted_iota(jnp.int32, (8, 8), 0) == lax.broadcasted_iota(jnp.int32, (8, 8), 1)
 
@@ -128,28 +136,32 @@
     pk[6:8, 0:512] = jnp.zeros((2, 512), F32)
     pk[:, 512:640] = jnp.broadcast_to(column(sb), (8, 128))
     pk[:, 640:768] = jnp.broadcast_to(column(dr), (8, 128))
+
+    half = lax.broadcasted_iota(jnp.int32, (2 * TOK, 256), 0) // TOK == c
+    for s in range(2):
+        v = step[s].astype(F32)
+        v = jnp.where(half, jnp.concatenate([v, v], axis=0), 0.0)
+        stt[s] = v.T.astype(BF16)
+
+    def send_step(i, carry):
+        d = peer(i)
+        pltpu.make_async_remote_copy(
+            st_src(d), stin.at[h], sstep, rstep, device_id=(z, d), device_id_type=MESH
+        ).start()
+        return carry
+
+    pl.semaphore_wait(barrier, NHEAD - 1 + NSEQ - 1)
     pltpu.make_async_copy(pk, pkall.at[r], rpar).start()
     for i in range(1, 4):
         pltpu.make_async_remote_copy(
             pk, pkall.at[r], spar, rpar, device_id=(z, g * 4 + lax.rem(r + i, 4)), device_id_type=MESH
         ).start()
-
-    half = lax.broadcasted_iota(jnp.int32, (2 * TOK, 256), 0) // TOK == c
-    for s in range(2):
-        v = step[s].astype(F32)
-        v = jnp.where(half, jnp.concatenate([v, v], axis=0), 0.0)
-        stt[s] = v.T.astype(BF16)
     pltpu.make_async_copy(st_src(h), stin.at[h], rstep).start()
-
-    def send_step(i, carry):
-        d = peer(i)
-        pltpu.make_async_remote_copy(
-            st_src(d), stin.at[h], sstep, rstep, device_id=(z, d), device_id_type=MESH
-        ).start()
-        return carry
-
     lax.fori_loop(1, NHEAD, send_step, 0)
-    send_x(1)
+    pltpu.make_async_copy(map_src(h), map_dst, rmap).start()
+    lax.fori_loop(1, NHEAD, send_map, 0)
+    for b in range(BATCH):
+        send_x(b)
 
     def done(ref, sem):
         pltpu.make_async_copy(ref, ref, sem).wait()
@@ -227,7 +239,6 @@
         return carry
 
     lax.fori_loop(0, SPANS, rows_of, 0)
-    send_x(2)
 
     done(mapin.at[pl.ds(EDGE, LEN), :], rmap)
     edge(mapin, shm, rhm).start()
@@ -245,11 +256,10 @@
         return carry
 
     lax.fori_loop(0, SPANS, map_span, 0)
-    pltpu.make_async_remote_copy(
+    sibling = pltpu.make_async_remote_copy(
         mapc.at[c], mapc.at[c], ssib, rsib, device_id=(z, g * 4 + seq * 2 + 1 - c), device_id_type=MESH
-    ).start()
-    done(mapc.at[1 - c], rsib)
-    send_x(3)
+    )
+    sibling.start()
 
     causal = lax.broadcasted_iota(jnp.int32, (SPAN, SPAN), 0) >= lax.broadcasted_iota(
         jnp.int32, (SPAN, SPAN), 1
@@ -261,50 +271,76 @@
         sc[k] = jnp.where(causal, dot(mapc[1, at, :], bt[k]), 0.0)
         return carry
 
-    lax.fori_loop(0, SPANS, scores, 0)
 
     row_id = lax.broadcasted_iota(jnp.int32, (32, CH), 0)
     same = lax.rem(row_id, 4) == lax.broadcasted_iota(jnp.int32, (32, CH), 1) // 64
     pick_scale = (same & (row_id >= 8) & (row_id < 16)).astype(BF16)
     pick_decay = (same & (row_id >= 16) & (row_id < 28)).astype(BF16)
-    low_lanes = lax.broadcasted_iota(jnp.int32, (SPAN, 128), 1) < 64
+    low_lanes = lax.broadcasted_iota(jnp.int32, (SPAN // 2, 128), 1) < 64
 
     def params_of(b):
         return pkall.at[2 * c + b // 2, :, cols(lax.rem(b, 2) * CH)]
 
-    def states(b):
+    def convolve(b):
         two = lax.rem(b, 2)
-        done(xin.at[b, pl.ds(EDGE, LEN), :], rx.at[b])
-        edge(xin.at[b], shx, rhx.at[b]).start()
-        done(xin.at[b, pl.ds(0, EDGE), :], rhx.at[b])
-        first_block(xin.at[b])
         par = params_of(b)
         weight = par[0:4, :]
         bias = par[4:5, :]
-        hc[...] = jnp.zeros_like(hc)
-        wrow[two, 0] = jnp.ones((8, CH), F32)
+        done(xin.at[b, pl.ds(EDGE, LEN), :], rx.at[b])
+        edge(xin.at[b], shx, rhx.at[b]).start()
+
+        def store(start, lanes, value):
+            xi[two, pl.ds(start, 64), lanes] = value
 
         def span(k, carry):
-            def store(start, lanes, value):
-                xi[two, pl.ds(start, 64), lanes] = value
-
             conv(xin.at[b], k, weight, bias, store)
+            return carry
+
+        lax.fori_loop(1, SPANS, span, 0)
+        done(xin.at[b, pl.ds(0, EDGE), :], rhx.at[b])
+        first_block(xin.at[b])
+        span(0, 0)
+
+    def states(b):
+        two = lax.rem(b, 2)
+
+        def produce(k):
             at = pl.ds(pl.multiple_of(k * SPAN, SPAN), SPAN)
             stack = rs[k, b].T.astype(BF16)
             scale = dot(stack, pick_scale)
             growth = dot(stack[SPAN - 16 :], pick_decay)[15:16]
             carried = (xi[two, at, :].astype(F32) * scale).astype(BF16)
-            produced = dot(bt[k], carried)
-            state = hc[...]
-            hs[two, k] = state
-            hc[...] = growth * state + produced
-            wrow[two, k + 1] = wrow[two, k] * growth
-            return carry
-
-        lax.fori_loop(0, SPANS, span, 0)
-        for j in range(NSEQ):
-            zs1[b * NSEQ + j, 0:32, :] = hc[j * 32 : (j + 1) * 32, :]
-            zs1[b * NSEQ + j, 32:40, :] = wrow[two, SPANS]
+            hs[two, k] = dot(bt[k], carried)
+            grow[k] = jnp.broadcast_to(growth, (8, CH))
+
+        def spans(i, carry):
+            produce(2 * i)
+            produce(2 * i + 1)
+            return carry
+
+        lax.fori_loop(0, SPANS // 2, spans, 0)
+        total = jnp.ones((8, CH), F32)
+        for k in range(SPANS):
+            wrow[two, k] = total
+            total = total * grow[k]
+        first, second, third = split(total[0:1])
+        line = lax.broadcasted_iota(jnp.int32, (16, CH), 0)
+        growth_rows = jnp.where(
+            line == 0, first, jnp.where(line == 1, second, jnp.where(line == 2, third, 0.0))
+        ).astype(BF16)
+
+        def scan(j, carry):
+            part = pl.ds(pl.multiple_of(j * 32, 32), 32)
+            state = jnp.zeros((32, CH), F32)
+            for k in range(SPANS):
+                made = hs[two, k, part, :]
+                hs[two, k, part, :] = state
+                state = grow[k, 0:1] * state + made
+            zs1[b * NSEQ + j, 0:32, :] = state.astype(BF16)
+            zs1[b * NSEQ + j, 32:48, :] = growth_rows
+            return carry
+
+        lax.fori_loop(0, NSEQ, scan, 0)
         pltpu.make_async_copy(zs1.at[b * NSEQ + z], zr1.at[b, z], rz1.at[b]).start()
 
         def send(i, carry):
@@ -320,8 +356,10 @@
         done(zr1.at[b], rz1.at[b])
         state = jnp.zeros((32, CH), F32)
         for j in range(NSEQ):
-            zs2[b * NSEQ + j] = state
-            state = zr1[b, j, 32:33, :] * state + zr1[b, j, 0:32, :]
+            zs2[b * NSEQ + j] = state.astype(BF16)
+            growth = zr1[b, j, 32:48, :].astype(F32)
+            growth = growth[0:1] + growth[1:2] + growth[2:3]
+            state = growth * state + zr1[b, j, 0:32, :].astype(F32)
         here = hin.at[b, pl.ds(pl.multiple_of(z * 32, 32), 32), :]
         pltpu.make_async_copy(zs2.at[b * NSEQ + z], here, rz2.at[b]).start()
 
@@ -334,76 +372,101 @@
 
         lax.fori_loop(1, NSEQ, send, 0)
 
+    HALF = SPAN // 2
+
     def within(b):
         two = lax.rem(b, 2)
         skip = params_of(b)[5:6, :]
 
-        def span(k, carry):
-            at = pl.ds(pl.multiple_of(k * SPAN, SPAN), SPAN)
+        def one_span(k):
             columns = rs[k, b, 0:8].T
-            own = sc[k]
             for pair in range(2):
                 lanes = slice(pair * 128, (pair + 1) * 128)
+                at = pl.ds(pl.multiple_of(k * SPAN, SPAN), SPAN)
                 x_pair = xi[two, at, lanes]
-                sums = []
+                early = []
+                late = []
                 for one in range(2):
                     i = pair * 2 + one
-                    exponent = columns[:, i : i + 1] + b2[k, b, i : i + 1]
-                    weights = (jnp.exp2(jnp.minimum(exponent, CAP)) * own).astype(BF16)
-                    sums.append(dot(weights, x_pair))
-                intra[two, at, lanes] = (
-                    jnp.where(low_lanes, sums[0], sums[1]) + skip[:, lanes] * x_pair.astype(F32)
+                    row = b2[k, b, i : i + 1]
+                    a_early = columns[:HALF, i : i + 1]
+                    a_late = columns[HALF:, i : i + 1]
+                    w = jnp.exp2(jnp.minimum(a_early + row[:, :HALF], CAP)) * sc[k, :HALF, :HALF]
+                    early.append(dot(w.astype(BF16), x_pair[:HALF]))
+                    w_old = jnp.exp2(a_late + row[:, :HALF]) * sc[k, HALF:, :HALF]
+                    w_own = jnp.exp2(jnp.minimum(a_late + row[:, HALF:], CAP)) * sc[k, HALF:, HALF:]
+                    w = jnp.concatenate([w_old.astype(BF16), w_own.astype(BF16)], axis=1)
+                    late.append(dot(w, x_pair))
+                direct = skip[:, lanes] * x_pair.astype(F32)
+                start = pl.multiple_of(k * SPAN, SPAN)
+                intra[two, pl.ds(start, HALF), lanes] = (
+                    jnp.where(low_lanes, early[0], early[1]) + direct[:HALF]
                 )
-            return carry
-
-        lax.fori_loop(0, SPANS, span, 0)
+                intra[two, pl.ds(start + HALF, HALF), lanes] = (
+                    jnp.where(low_lanes, late[0], late[1]) + direct[HALF:]
+                )
+
+        def spans(i, carry):
+            one_span(2 * i)
+            one_span(2 * i + 1)
+            return carry
+
+        lax.fori_loop(0, SPANS // 2, spans, 0)
 
     def finish(b):
         two = lax.rem(b, 2)
         done(hin.at[b], rz2.at[b])
 
-        def span(i, carry):
-            k = lax.rem(g + i, SPANS)
+        def span(k):
             at = pl.ds(pl.multiple_of(k * SPAN, SPAN), SPAN)
-            entering = (hs[two, k] + wrow[two, k, 0:1] * hin[b]).astype(BF16)
+            entering = (hs[two, k] + wrow[two, k, 0:1] * hin[b].astype(F32)).astype(BF16)
             inter = dot(mapc[1, at, :], entering)
             decay = dot(rs[k, b].T.astype(BF16), pick_decay)
             ob[b, at, :] = (intra[two, at, :] + decay * inter).astype(BF16)
-            for j in range(4):
-                d = k * 4 + lax.rem(r + j, 4)
-                src = ob.at[b, rows(d * TOK, TOK), :]
-                dst = out.at[seq, :, cols(hb * 1024 + b * CH)]
-
-                @pl.when(d == h)
-                def _():
-                    pltpu.make_async_copy(src, dst, rout).start()
-
-                @pl.when(d != h)
-                def _():
-                    pltpu.make_async_remote_copy(
-                        src, dst, sout, rout, device_id=(z, d), device_id_type=MESH
-                    ).start()
-
-            return carry
-
-        lax.fori_loop(0, SPANS, span, 0)
+
+        def spans(i, carry):
+            span(2 * i)
+            span(2 * i + 1)
+            return carry
+
+        lax.fori_loop(0, SPANS // 2, spans, 0)
+        dst = out.at[seq, :, cols(hb * 1024 + b * CH)]
+
+        def leave(i, carry):
+            d = peer(i)
+            pltpu.make_async_remote_copy(
+                ob.at[b, rows(d * TOK, TOK), :], dst, sout, rout, device_id=(z, d), device_id_type=MESH
+            ).start()
+            return carry
+
+        pltpu.make_async_copy(ob.at[b, rows(h * TOK, TOK), :], dst, rout).start()
+        lax.fori_loop(1, NHEAD, leave, 0)
 
     def turn(i, carry):
+        @pl.when(i > 0)
+        def _():
+            relay(i - 1)
+
         @pl.when(i < BATCH)
         def _():
+            convolve(i)
+
+        @pl.when(i == 0)
+        def _():
+            done(mapc.at[1 - c], rsib)
+            lax.fori_loop(0, SPANS, scores, 0)
+
+        @pl.when(i < BATCH)
+        def _():
             states(i)
 
         @pl.when(i > 0)
         def _():
-            relay(i - 1)
+            finish(i - 1)
 
         @pl.when(i < BATCH)
         def _():
             within(i)
-
-        @pl.when(i > 0)
-        def _():
-            finish(i - 1)
 
         return carry
 
@@ -424,10 +487,17 @@
 
 
 def local(proj, maps, step, sb, dr, sg, cw, cb, mw, mb):
-    vmem = pl.BlockSpec(memory_space=pltpu.VMEM)
-    hbm = pl.BlockSpec(memory_space=pl.ANY)
+    hbm = pl.BlockSpec(memory_space=pltpu.HBM)
     dma = pltpu.SemaphoreType.DMA
     scratch = [
+        pltpu.VMEM(step.shape, BF16),
+        pltpu.VMEM((1, 8), F32),
+        pltpu.VMEM((1, 8), F32),
+        pltpu.VMEM((1, 8), F32),
+        pltpu.VMEM(cw.shape, BF16),
+        pltpu.VMEM((1, 512), F32),
+        pltpu.VMEM(mw.shape, BF16),
+        pltpu.VMEM((1, 4096), F32),
         pltpu.VMEM((BATCH, EDGE + LEN, CH), BF16),
         pltpu.VMEM((EDGE + LEN, CH), BF16),
         pltpu.VMEM((2, LEN, CH), BF16),
@@ -435,7 +505,6 @@
         pltpu.VMEM((SPANS, SPAN, SPAN), F32),
         pltpu.VMEM((2, LEN, CH), BF16),
         pltpu.VMEM((2, SPANS, 256, CH), F32),
-        pltpu.VMEM((256, CH), F32),
         pltpu.VMEM((2, LEN, CH), F32),
         pltpu.VMEM((BATCH, LEN, CH), BF16),
         pltpu.VMEM((2, 64 + EDGE, 128), F32),
@@ -449,21 +518,22 @@
         pltpu.VMEM((7, 16, SPAN), F32),
         pltpu.VMEM((SPANS, BATCH, 32, SPAN), F32),
         pltpu.VMEM((SPANS, BATCH, 8, SPAN), F32),
-        pltpu.VMEM((BATCH * NSEQ, 40, CH), F32),
-        pltpu.VMEM((BATCH, NSEQ, 40, CH), F32),
-        pltpu.VMEM((BATCH * NSEQ, 32, CH), F32),
-        pltpu.VMEM((BATCH, 256, CH), F32),
-        pltpu.VMEM((2, SPANS + 1, 8, CH), F32),
+        pltpu.VMEM((BATCH * NSEQ, 48, CH), BF16),
+        pltpu.VMEM((BATCH, NSEQ, 48, CH), BF16),
+        pltpu.VMEM((BATCH * NSEQ, 32, CH), BF16),
+        pltpu.VMEM((BATCH, 256, CH), BF16),
+        pltpu.VMEM((2, SPANS, 8, CH), F32),
+        pltpu.VMEM((SPANS, 8, CH), F32),
     ]
-    scratch += [dma((BATCH,))] * 4 + [dma] * 16
+    scratch += [dma((8,))] + [dma((BATCH,))] * 4 + [dma] * 16
     return pl.pallas_call(
         kernel,
         out_shape=jax.ShapeDtypeStruct(proj.shape, BF16),
-        in_specs=[hbm, hbm] + [vmem] * 8,
-        out_specs=hbm,
+        in_specs=[hbm] * 10,
+        out_specs=pl.BlockSpec(memory_space=pl.ANY),
         scratch_shapes=scratch,
         compiler_params=pltpu.CompilerParams(
-            collective_id=0, has_side_effects=True, vmem_limit_bytes=48 * 1024 * 1024
+            collective_id=0, has_side_effects=True, vmem_limit_bytes=62 * 1024 * 1024
         ),
     )(
         proj, maps, step, sb.reshape(1, -1), dr.reshape(1, -1), sg.reshape(1, -1),

time: 196 us -> 121 us (0.62)
  the two profiles are of different devices: /device:TPU:93 before, /device:TPU:1 now
where the time goes in v2:
time: 121 us
  Pallas kernels  116 us (96%)
  local copies, waits for them, and re-layouts  4.57 us (4%)
    pallas_call x1, Pallas kernels, local(): pl.pallas_call(kernel, out_shape=jax.ShapeDtypeStruct(proj.shape, BF16),...  116 us
    unnamed x1, local copies, waits for them, and re-layouts  4.57 us

profile of v2, /device:TPU:1, one launch (start us, length us, event | category | flops | bytes accessed | tf_op | source)
XLA Modules:
  0.0 120.9 jit_solution(11980575317464660314)
XLA Ops:
  0.0 116.3 %shard_map.100 = bf16[2,64,16384]{2,1,0:T(8,128)(2,1)} custom-call(bf16[2,64,16384]{2,1,0:T(8,128)(2,1)} %proj.1, bf16[2,64,4096]{2,1,0:T(8,128)(2,1)} %maps.1, bf16[2,64,256]{2,1,0:T(8,128)(2,1)} %step_in.1, f32[1,8]{1,0:T(1,128)} %bitcast.7, f32[1,8]{1,0:T(1,128)} %bitcast.8, f32[1,8]{1,0:T(1,128)} %bitcast.9, bf16[4,512]{1,0:T(4,128)(2,1)} %cw_in.1, ...), custom_call_target="tpu_custom_call" | custom-call | tf_op jit(solution)/shard_map/pallas_call | solution.py:529
  116.4 4.6 %copy.12 = bf16[2,64,16384]{2,1,0:T(8,128)(2,1)} copy(bf16[2,64,16384]{2,1,0:T(8,128)(2,1)} %shard_map.100) | data formatting | bytes 8388608

commit v3 on v2

--- a/solution.py
+++ b/solution.py
@@ -526,6 +526,7 @@
         pltpu.VMEM((SPANS, 8, CH), F32),
     ]
     scratch += [dma((8,))] + [dma((BATCH,))] * 4 + [dma] * 16
+    pin = lambda a: pltpu.with_memory_space_constraint(a, pltpu.HBM)
     return pl.pallas_call(
         kernel,
         out_shape=jax.ShapeDtypeStruct(proj.shape, BF16),
@@ -533,11 +534,11 @@
         out_specs=pl.BlockSpec(memory_space=pl.ANY),
         scratch_shapes=scratch,
         compiler_params=pltpu.CompilerParams(
-            collective_id=0, has_side_effects=True, vmem_limit_bytes=62 * 1024 * 1024
+            collective_id=0, has_side_effects=True, vmem_limit_bytes=48 * 1024 * 1024
         ),
     )(
-        proj, maps, step, sb.reshape(1, -1), dr.reshape(1, -1), sg.reshape(1, -1),
-        cw, cb.reshape(1, -1), mw, mb.reshape(1, -1),
+        *[pin(a) for a in (proj, maps, step, sb.reshape(1, -1), dr.reshape(1, -1), sg.reshape(1, -1),
+        cw, cb.reshape(1, -1), mw, mb.reshape(1, -1))],
     )
 
 

time: 121 us -> 118 us (0.975)
  local copies, waits for them, and re-layouts: 4.57 us -> 2.02 us
    unnamed x1, local copies, waits for them, and re-layouts: 4.57 us -> 2.02 us
where the time goes in v3:
time: 118 us
  Pallas kernels  116 us (98%)
  local copies, waits for them, and re-layouts  2.02 us (2%)
    pallas_call x1, Pallas kernels, local(): pl.pallas_call(kernel, out_shape=jax.ShapeDtypeStruct(proj.shape, BF16),...  116 us

profile of v3, /device:TPU:1, one launch (start us, length us, event | category | flops | bytes accessed | tf_op | source)
XLA Modules:
  0.0 118.3 jit_solution(8417061717146929914)
XLA Ops:
  0.0 116.2 %shard_map.100 = bf16[2,64,16384]{2,1,0:T(8,128)(2,1)S(1)} custom-call(bf16[2,64,16384]{2,1,0:T(8,128)(2,1)} %proj.1, bf16[2,64,4096]{2,1,0:T(8,128)(2,1)} %maps.1, bf16[2,64,256]{2,1,0:T(8,128)(2,1)} %step_in.1, f32[1,8]{1,0:T(1,128)} %bitcast.7, f32[1,8]{1,0:T(1,128)} %bitcast.8, f32[1,8]{1,0:T(1,128)} %bitcast.9, bf16[4,512]{1,0:T(4,128)(2,1)} %cw_in.1, ...), custom_call_target="tpu_custom_call" | custom-call | tf_op jit(solution)/shard_map/pallas_call | solution.py:530
  116.2 2.0 %copy.12 = bf16[2,64,16384]{2,1,0:T(8,128)(2,1)} copy(bf16[2,64,16384]{2,1,0:T(8,128)(2,1)S(1)} %shard_map.100) | data formatting | bytes 8388608

commit v4 on v3

--- a/solution.py
+++ b/solution.py
@@ -72,6 +72,44 @@
 
     lax.fori_loop(1, NHEAD, greet, 0)
     lax.fori_loop(1, NSEQ, greet_z, 0)
+    def cols(start, width=CH):
+        return pl.ds(pl.multiple_of(start, 128), width)
+
+    def rows(start, count):
+        return pl.ds(pl.multiple_of(start, 16), count)
+
+    def map_src(d):
+        return maps.at[lax.rem(d // 2, 2), :, cols(lax.rem(d, 2) * 2048 + (d // 4) * 256)]
+
+    def x_src(d, b):
+        base = ((d // 4) * 2 + lax.rem(d, 2)) * 1024
+        return proj.at[lax.rem(d // 2, 2), :, cols(base + b * CH)]
+
+    def st_src(d):
+        return stt.at[lax.rem(d // 2, 2), rows(((d // 4) * 2 + lax.rem(d, 2)) * 16, 16), :]
+
+    map_dst = mapin.at[rows(EDGE + h * TOK, TOK), :]
+
+    def send_map(i, carry):
+        d = peer(i)
+        pltpu.make_async_remote_copy(
+            map_src(d), map_dst, smap, rmap, device_id=(z, d), device_id_type=MESH
+        ).start()
+        return carry
+
+    def send_x(b):
+        dst = xin.at[b, rows(EDGE + h * TOK, TOK), :]
+        pltpu.make_async_copy(x_src(h, b), dst, rx.at[b]).start()
+
+        def one(i, carry):
+            d = peer(i)
+            pltpu.make_async_remote_copy(
+                x_src(d, b), dst, sx, rx.at[b], device_id=(z, d), device_id_type=MESH
+            ).start()
+            return carry
+
+        lax.fori_loop(1, NHEAD, one, 0)
+
     arrivals = [
         pltpu.make_async_copy(src, dst, small.at[i])
         for i, (src, dst) in enumerate(
@@ -81,46 +119,11 @@
     ]
     for arrival in arrivals:
         arrival.start()
+    pl.semaphore_wait(barrier, NHEAD - 1 + NSEQ - 1)
+    pltpu.make_async_copy(map_src(h), map_dst, rmap).start()
+    lax.fori_loop(1, NHEAD, send_map, 0)
     for arrival in arrivals:
         arrival.wait()
-
-    def cols(start, width=CH):
-        return pl.ds(pl.multiple_of(start, 128), width)
-
-    def rows(start, count):
-        return pl.ds(pl.multiple_of(start, 16), count)
-
-    def map_src(d):
-        return maps.at[lax.rem(d // 2, 2), :, cols(lax.rem(d, 2) * 2048 + (d // 4) * 256)]
-
-    def x_src(d, b):
-        base = ((d // 4) * 2 + lax.rem(d, 2)) * 1024
-        return proj.at[lax.rem(d // 2, 2), :, cols(base + b * CH)]
-
-    def st_src(d):
-        return stt.at[lax.rem(d // 2, 2), rows(((d // 4) * 2 + lax.rem(d, 2)) * 16, 16), :]
-
-    map_dst = mapin.at[rows(EDGE + h * TOK, TOK), :]
-
-    def send_map(i, carry):
-        d = peer(i)
-        pltpu.make_async_remote_copy(
-            map_src(d), map_dst, smap, rmap, device_id=(z, d), device_id_type=MESH
-        ).start()
-        return carry
-
-    def send_x(b):
-        dst = xin.at[b, rows(EDGE + h * TOK, TOK), :]
-        pltpu.make_async_copy(x_src(h, b), dst, rx.at[b]).start()
-
-        def one(i, carry):
-            d = peer(i)
-            pltpu.make_async_remote_copy(
-                x_src(d, b), dst, sx, rx.at[b], device_id=(z, d), device_id_type=MESH
-            ).start()
-            return carry
-
-        lax.fori_loop(1, NHEAD, one, 0)
 
     eye = lax.broadcasted_iota(jnp.int32, (8, 8), 0) == lax.broadcasted_iota(jnp.int32, (8, 8), 1)
 
@@ -150,7 +153,6 @@
         ).start()
         return carry
 
-    pl.semaphore_wait(barrier, NHEAD - 1 + NSEQ - 1)
     pltpu.make_async_copy(pk, pkall.at[r], rpar).start()
     for i in range(1, 4):
         pltpu.make_async_remote_copy(
@@ -158,8 +160,6 @@
         ).start()
     pltpu.make_async_copy(st_src(h), stin.at[h], rstep).start()
     lax.fori_loop(1, NHEAD, send_step, 0)
-    pltpu.make_async_copy(map_src(h), map_dst, rmap).start()
-    lax.fori_loop(1, NHEAD, send_map, 0)
     for b in range(BATCH):
         send_x(b)
 
@@ -341,8 +341,6 @@
             return carry
 
         lax.fori_loop(0, NSEQ, scan, 0)
-        pltpu.make_async_copy(zs1.at[b * NSEQ + z], zr1.at[b, z], rz1.at[b]).start()
-
         def send(i, carry):
             d = zpeer(i)
             pltpu.make_async_remote_copy(
@@ -350,13 +348,18 @@
             ).start()
             return carry
 
-        lax.fori_loop(1, NSEQ, send, 0)
+        @pl.when(z < NSEQ - 1)
+        def _():
+            pltpu.make_async_copy(zs1.at[b * NSEQ + z], zr1.at[b, z], rz1.at[b]).start()
+            lax.fori_loop(1, NSEQ, send, 0)
 
     def relay(b):
-        done(zr1.at[b], rz1.at[b])
+        done(zr1.at[b, pl.ds(0, NSEQ - 1)], rz1.at[b])
         state = jnp.zeros((32, CH), F32)
         for j in range(NSEQ):
             zs2[b * NSEQ + j] = state.astype(BF16)
+            if j == NSEQ - 1:
+                break
             growth = zr1[b, j, 32:48, :].astype(F32)
             growth = growth[0:1] + growth[1:2] + growth[2:3]
             state = growth * state + zr1[b, j, 0:32, :].astype(F32)
@@ -480,7 +483,11 @@
     done(xin.at[0, pl.ds(0, BATCH * EDGE), :], shx)
     done(mapin.at[pl.ds(0, EDGE), :], shm)
     done(mapc.at[0], ssib)
-    done(zs1.at[pl.ds(0, BATCH * (NSEQ - 1))], sz1)
+
+    @pl.when(z < NSEQ - 1)
+    def _():
+        done(zs1.at[pl.ds(0, BATCH * (NSEQ - 1))], sz1)
+
     done(zs2.at[pl.ds(0, BATCH * (NSEQ - 1))], sz2)
     done(out.at[:, :, pl.ds(0, most)], sout)
     done(out, rout)

time: 118 us -> 118 us (level)
  no operation moved by 1% of the time
where the time goes in v4:
time: 118 us
  Pallas kernels  116 us (98%)
  local copies, waits for them, and re-layouts  2.02 us (2%)
    pallas_call x1, Pallas kernels, local(): pl.pallas_call(kernel, out_shape=jax.ShapeDtypeStruct(proj.shape, BF16),...  116 us

profile of v4, /device:TPU:1, one launch (start us, length us, event | category | flops | bytes accessed | tf_op | source)
XLA Modules:
  0.0 117.8 jit_solution(8998424166005276241)
XLA Ops:
  0.0 115.7 %shard_map.100 = bf16[2,64,16384]{2,1,0:T(8,128)(2,1)S(1)} custom-call(bf16[2,64,16384]{2,1,0:T(8,128)(2,1)} %proj.1, bf16[2,64,4096]{2,1,0:T(8,128)(2,1)} %maps.1, bf16[2,64,256]{2,1,0:T(8,128)(2,1)} %step_in.1, f32[1,8]{1,0:T(1,128)} %bitcast.7, f32[1,8]{1,0:T(1,128)} %bitcast.8, f32[1,8]{1,0:T(1,128)} %bitcast.9, bf16[4,512]{1,0:T(4,128)(2,1)} %cw_in.1, ...), custom_call_target="tpu_custom_call" | custom-call | tf_op jit(solution)/shard_map/pallas_call | solution.py:537
  115.7 2.0 %copy.12 = bf16[2,64,16384]{2,1,0:T(8,128)(2,1)} copy(bf16[2,64,16384]{2,1,0:T(8,128)(2,1)S(1)} %shard_map.100) | data formatting | bytes 8388608
